TPU v7x, 32 devices: a whole 2x2x4 slice. The times are simulated.
32 devices in a mesh: row: 4 (over y, x), col: 8 (over z, core).
Axes of the slice: x: 2, y: 2, z: 4, core: 2. Of those that a mesh axis runs over, the one named last changes fastest.
Arguments:
- root_inverse: bfloat16 [4096, 4096], P('row', 'col'), may hold values from -16 to 16
- factor: bfloat16 [4096, 4, 4096], P('row', None, 'col'), may hold values from -0.59765625 to 0.59765625
- inverse_diag: bfloat16 [4096, 4, 4096], P('row', None, 'col'), may hold values from -6 to 6
- structure: int32 [4, 32], replicated, may hold values 0 or 1
Outputs:
- ainv_rk: bfloat16 [4096, 4, 4096], P('row', None, 'col')
- ainv_kk: bfloat16 [4096, 4, 4096], P('row', None, 'col')
All inputs are finite; a program needn't handle non-finite values.
Results may differ from a plain program's by a relative error of at most 0.014.
Values may be sent and summed in bfloat16 or wider, within the bound.
A program may use at most 128 MiB of HBM per device.

v0:
```python
import jax
import jax.numpy as jnp
from jax import lax
from jax.sharding import PartitionSpec as P

BLK = 128


def body(root_inverse, factor, inverse_diag, structure):
    local_rows = factor.shape[0]
    offset = lax.axis_index("row") * local_rows
    row_mask = jnp.repeat(structure, BLK, axis=1)
    local_mask = lax.dynamic_slice_in_dim(row_mask, offset, local_rows, 1).T.astype(factor.dtype)
    masked = factor * local_mask[:, :, None]
    masked_rows = lax.all_gather(masked, "col", axis=2, tiled=True)
    root_rows = lax.all_gather(root_inverse, "col", axis=1, tiled=True)
    product = jnp.einsum(
        "ik,knj->inj",
        root_rows,
        lax.all_gather(masked, "row", axis=0, tiled=True),
        preferred_element_type=jnp.float32,
    )
    ainv_rk = (-product).astype(jnp.bfloat16)
    running = lax.psum_scatter(
        jnp.einsum("kni,knj->inj", masked_rows, ainv_rk, preferred_element_type=jnp.float32).astype(
            jnp.bfloat16
        ),
        "row",
        scatter_dimension=0,
        tiled=True,
    ).astype(jnp.float32)
    ainv_kk = (inverse_diag.astype(jnp.float32) - running).astype(jnp.bfloat16)
    return (ainv_rk, ainv_kk)


def solution(mesh):
    return jax.shard_map(
        body,
        mesh=mesh,
        in_specs=(P("row", "col"), P("row", None, "col"), P("row", None, "col"), P()),
        out_specs=(P("row", None, "col"), P("row", None, "col")),
        check_vma=False,
    )
```

profile of v0, /device:TPU:7, one launch (start us, length us, event | category | flops | bytes accessed | tf_op | source)
XLA Modules:
  0.0 740.6 jit_solution(15655745726351984514)
XLA Ops:
  7.2 0.0 copy-start
  7.2 0.0 all-gather.6.cloned.1.call-start
  7.2 0.7 all-gather.6.cloned.1.call-update
  7.9 0.0 all-gather.4.cloned.1.call-start
  8.0 0.0 copy-done
  8.0 0.1 broadcast_bitcast_fusion
  8.1 0.1 copy.14
  8.1 7.4 %copy.6 = bf16[1024,4,512]{0,2,1:T(8,128)(2,1)} copy(bf16[1024,4,512]{2,1,0:T(4,128)(2,1)} %param.5) | data formatting | bytes 8388608 | tf_op args[1]
  15.5 4.5 broadcast_multiply_fusion
  20.0 0.0 all-gather.4.cloned.1.call-update
  20.1 0.0 all-gather.8.cloned.1.call-start
  20.1 0.7 all-gather.8.cloned.1.call-update
  20.8 0.0 reduce-scatter.2.cloned.1.call-start
  20.8 72.5 %all-gather.6.cloned.1.call-done = bf16[1024,4096]{1,0:T(8,128)(2,1)} async-done(((bf16[1024,512]{1,0:T(8,128)(2,1)}), bf16[1024,4096]{1,0:T(8,128)(2,1)}) %all-gather.6.cloned.1.call-update) | async-done | bytes 8388624 | tf_op jit(solution)/shard_map/all_gather | solution.py:16
  93.3 157.1 %all-gather.4.cloned.1.call-done = bf16[4096,4,512]{0,2,1:T(8,128)(2,1)} async-done(((bf16[1024,4,512]{0,2,1:T(8,128)(2,1)}), bf16[4096,4,512]{0,2,1:T(8,128)(2,1)}) %all-gather.4.cloned.1.call-update) | async-done | bytes 16777232 | tf_op jit(solution)/shard_map/all_gather | solution.py:20
  250.4 23.8 %fusion.2 = bf16[1024,4,512]{0,2,1:T(8,128)(2,1)} fusion(bf16[4096,4,512]{0,2,1:T(8,128)(2,1)} %all-gather.4.cloned.1.call-done, bf16[1024,4096]{1,0:T(8,128)(2,1)} %all-gather.6.cloned.1.call-done), kind=kOutput, calls=%fused_computation.5 | convolution fusion | flops 17184063488 | bytes 29360128 | tf_op jit(solution)/shard_map/ik,knj->inj/dot_general | solution.py:17
  274.1 268.4 %all-gather.8.cloned.1.call-done = bf16[1024,4,4096]{0,2,1:T(8,128)(2,1)} async-done(((bf16[1024,4,512]{0,2,1:T(8,128)(2,1)}), bf16[1024,4,4096]{0,2,1:T(8,128)(2,1)}) %all-gather.8.cloned.1.call-update) | async-done | bytes 33554448 | tf_op jit(solution)/shard_map/all_gather | solution.py:15
  542.6 25.3 %convert_bitcast_fusion = bf16[4096,4,512]{0,2,1:T(8,128)(2,1)} fusion(bf16[1024,4,512]{0,2,1:T(8,128)(2,1)} %fusion.2, bf16[1024,4,4096]{0,2,1:T(8,128)(2,1)} %all-gather.8.cloned.1.call-done), kind=kOutput, calls=%fused_computation | convolution fusion | flops 17188257792 | bytes 54525952 | tf_op jit(solution)/shard_map/kni,knj->inj/dot_general | solution.py:25
  567.9 0.0 reduce-scatter.2.cloned.1.call-update
  567.9 7.5 %copy.7 = bf16[1024,4,512]{0,2,1:T(8,128)(2,1)} copy(bf16[1024,4,512]{2,1,0:T(4,128)(2,1)} %param.6) | data formatting | bytes 8388608 | tf_op args[2]
  575.4 0.0 copy-start.1
  575.4 7.9 %copy.9 = bf16[1024,4,512]{2,1,0:T(4,128)(2,1)} copy(bf16[1024,4,512]{0,2,1:T(8,128)(2,1)} %fusion.2) | data formatting | bytes 8388608
  583.4 135.3 %reduce-scatter.2.cloned.1.call-done = bf16[1024,4,512]{0,2,1:T(8,128)(2,1)} async-done(((bf16[4096,4,512]{0,2,1:T(8,128)(2,1)}), bf16[1024,4,512]{0,2,1:T(8,128)(2,1)}) %reduce-scatter.2.cloned.1.call-update) | async-done | bytes 4194320 | tf_op jit(solution)/shard_map/reduce_scatter | solution.py:24
  718.6 7.6 %subtract_convert_fusion = bf16[1024,4,512]{0,2,1:T(8,128)(2,1)} fusion(bf16[1024,4,512]{0,2,1:T(8,128)(2,1)} %reduce-scatter.2.cloned.1.call-done, bf16[1024,4,512]{0,2,1:T(8,128)(2,1)} %copy.7), kind=kLoop, calls=%fused_computation.3 | loop fusion | flops 8388608 | bytes 12582912 | tf_op jit(solution)/shard_map/convert_element_type | solution.py:32
  726.2 7.8 %copy.10 = bf16[1024,4,512]{2,1,0:T(4,128)(2,1)} copy(bf16[1024,4,512]{0,2,1:T(8,128)(2,1)} %subtract_convert_fusion) | data formatting | bytes 8388608
  734.0 0.0 copy-done.1
  (1 shorter events, 0.0 us)
Async XLA Ops:
  7.2 0.8 copy-start
  7.2 86.1 %all-gather.6.cloned.1.call-start = ((), (), s32[]{:S(2)}) async-start(), calls=%async_computation.2 | async-start | bytes 9437184 | tf_op jit(solution)/shard_map/all_gather | solution.py:16
  7.9 242.5 %all-gather.4.cloned.1.call-start = ((), (), s32[]{:S(2)}) async-start(), calls=%async_computation.1 | async-start | bytes 20971520 | tf_op jit(solution)/shard_map/all_gather | solution.py:20
  20.1 522.5 %all-gather.8.cloned.1.call-start = ((), (), s32[]{:S(2)}) async-start(), calls=%async_computation.3 | async-start | bytes 37748736 | tf_op jit(solution)/shard_map/all_gather | solution.py:15
  20.8 697.9 %reduce-scatter.2.cloned.1.call-start = ((), (), s32[]{:S(2)}) async-start(), calls=%async_computation.4 | async-start | bytes 20971520 | tf_op jit(solution)/shard_map/reduce_scatter | solution.py:24
  575.4 158.6 %copy-start.1 = (s32[4,32]{1,0:T(4,128)S(1)}, s32[4,32]{1,0:T(4,128)}, u32[]{:S(2)}) copy-start(s32[4,32]{1,0:T(4,128)} %param.7) | copy-start | bytes 1540
Sparse Core Ops, SparseCore 0:
  9.6 83.6 all-gather.5
  95.7 154.6 all-gather.3
  252.6 289.9 all-gather.7
  568.0 150.5 reduce-scatter.1
where the time goes:
time: 744 us; the launch traced here: 741 us
  waiting for transfers between devices  635 us (85%)
  matrix products  49.1 us (7%)
  local copies, waits for them, and re-layouts  30.9 us (4%)
  between operations  13.8 us (2%)
  other arithmetic  12.1 us (2%)
    all_gather x1, waiting for transfers between devices, body(): masked_rows = lax.all_gather(masked, 'col', axis=2, tiled=True)  268 us
    all_gather x1, waiting for transfers between devices, body(): lax.all_gather(masked, 'row', axis=0, tiled=True)  157 us
    reduce_scatter x1, waiting for transfers between devices, body(): lax.psum_scatter(jnp.einsum('kni,knj->inj', masked_rows, ainv_rk, preferr...  135 us
    all_gather x1, waiting for transfers between devices, body(): root_rows = lax.all_gather(root_inverse, 'col', axis=1, tiled=True)  72.5 us
    unnamed x10, local copies, waits for them, and re-layouts  30.9 us
    dot_general x1, matrix products, body(): jnp.einsum('kni,knj->inj', masked_rows, ainv_rk, preferred_element_type=j...  25.3 us
    dot_general x1, matrix products, body(): jnp.einsum('ik,knj->inj', root_rows, lax.all_gather(masked, 'row', axis=0...  23.8 us
  transfers between devices with their start and end apart: 4, of which 4 were waited for; matrix products, arithmetic and copies ran while one was open for 7% of the time, Pallas kernels for 0%

commit v1 on v0

v1 whole, which is shorter than its diff:
```python
import functools

import jax
import jax.numpy as jnp
from jax import lax
from jax.experimental import pallas as pl
from jax.experimental.pallas import tpu as pltpu
from jax.sharding import PartitionSpec as P

BLK = 128
CORES = 2
MESH = pl.DeviceIdType.MESH


def kernel(
    n_row, n_col, root_in, m_in, p_out, t_out, m_line, m_plane,
    root, col_buf, chunk_buf, p_buf, pt_buf, part_buf, sum_buf, t_buf,
    own_sem, up_send, up_recv, down_send, down_recv, mate_send, mate_recv,
    plane_send, plane_recv, part_send, part_recv, load_sem, out_sem, t_sem,
):
    kids, rows, cols = m_in.shape
    n_z = n_col // CORES
    per_row = rows // cols
    r, c = lax.axis_index("row"), lax.axis_index("col")
    z, core = c // CORES, c % CORES
    mate = z * CORES + 1 - core

    barrier = pltpu.get_barrier_semaphore()

    def greet(dev):
        pl.semaphore_signal(barrier, inc=1, device_id=dev, device_id_type=MESH)

    greet((r, mate))
    for d in range(1, n_row):
        greet((lax.rem(r + d, n_row), c))

    for step in (1, n_z - 1):
        greet((r, lax.rem(z + step, n_z) * CORES + core))

    own = [
        pltpu.make_async_copy(root_in, root.at[c], own_sem.at[0]),
        pltpu.make_async_copy(m_in, m_line.at[:, c], own_sem.at[1]),
        pltpu.make_async_copy(m_in, m_plane.at[:, r], own_sem.at[2]),
    ]
    for copy in own:
        copy.start()
    for copy in own:
        copy.wait()

    pl.semaphore_wait(barrier, n_row + 2)

    def slot(item, at):
        return root.at[at] if isinstance(item, int) else m_line.at[item - 1, at]

    def up(item, h, at):
        ref = slot(item, at)
        return pltpu.make_async_remote_copy(
            ref, ref, up_send.at[item, h], up_recv.at[item, h], (r, c + CORES), MESH)

    def down(item, h, at):
        ref = slot(item, at)
        return pltpu.make_async_remote_copy(
            ref, ref, down_send.at[item, h], down_recv.at[item, h], (r, c - CORES), MESH)

    def share(item, zz, at):
        ref = slot(item, at)
        return pltpu.make_async_remote_copy(
            ref, ref, mate_send.at[item, zz], mate_recv.at[item, zz], (r, mate), MESH)

    def begin(item):
        @pl.when(z < n_z - 1)
        def _():
            up(item, 0, c).start()

        @pl.when(z > 0)
        def _():
            down(item, 0, c).start()

        share(item, z, c).start()

    def arrive(item, h):
        low, high = z - 1 - h, z + 1 + h

        @pl.when(low >= 0)
        def _():
            at = low * CORES + core
            up(item, h, at).wait_recv()

            @pl.when((z < n_z - 1) & (h < n_z - 2))
            def _():
                up(item, h + 1, at).start()

            share(item, low, at).start()

        @pl.when(high < n_z)
        def _():
            at = high * CORES + core
            down(item, h, at).wait_recv()

            @pl.when((z > 0) & (h < n_z - 2))
            def _():
                down(item, h + 1, at).start()

            share(item, high, at).start()

    def finish_line(item):
        def hop(h, _):
            @pl.when((z < n_z - 1) & (z - h >= 0))
            def _():
                up(item, h, c - h * CORES).wait_send()

            @pl.when((z > 0) & (z + h < n_z))
            def _():
                down(item, h, c + h * CORES).wait_send()

            return 0

        lax.fori_loop(0, n_z - 1, hop, 0)

        def mates(zz, _):
            share(item, zz, zz * CORES + core).wait_send()
            return 0

        lax.fori_loop(0, n_z, mates, 0)

    def to_row(n, d):
        ref = m_plane.at[n, r]
        return pltpu.make_async_remote_copy(
            ref, ref, plane_send.at[n, d - 1], plane_recv.at[n, d - 1],
            (lax.rem(r + d, n_row), c), MESH)

    def from_row(n, d):
        ref = m_plane.at[n, lax.rem(r - d + n_row, n_row)]
        return pltpu.make_async_remote_copy(
            ref, ref, plane_send.at[n, d - 1], plane_recv.at[n, d - 1],
            (lax.rem(r + d, n_row), c), MESH)

    def send_plane(n):
        for d in range(1, n_row):
            to_row(n, d).start()

    def part_copy(n, at):
        half = lax.rem(at, per_row)
        return pltpu.make_async_remote_copy(
            part_buf.at[n, at], sum_buf.at[n, r, half], part_send.at[n, at],
            part_recv.at[n, r, half], (at // per_row, c), MESH)

    def p_store(n):
        return pltpu.make_async_copy(p_buf, p_out.at[n], out_sem)

    def make_p(n):
        for d in range(1, n_row):
            from_row(n, d).wait_recv()
        load = pltpu.make_async_copy(m_plane.at[n], col_buf, load_sem.at[0])
        load.start()

        @pl.when(n > 0)
        def _():
            p_store(n - 1).wait()

        load.wait()
        tile = min(256, rows)

        def one(t, _):
            at = pl.ds(pl.multiple_of(t * tile, tile), tile)
            total = jnp.zeros((tile, cols), jnp.float32)
            for k in range(n_col):
                block = col_buf[k // per_row, pl.ds((k % per_row) * cols, cols), :]
                total += jnp.dot(root[k, at, :], block, preferred_element_type=jnp.float32)
            total = -total
            p_buf[at, :] = total.astype(p_buf.dtype)
            pt_buf[t, :, :] = total.T.astype(pt_buf.dtype)
            return 0

        lax.fori_loop(0, rows // tile, one, 0)
        p_store(n).start()

    def chunk_load(n, zz, i):
        return pltpu.make_async_copy(
            m_line.at[n, zz * CORES + i], chunk_buf.at[i], load_sem.at[1 + i])

    def consume(n, zz):
        for i in range(CORES):
            chunk_load(n, zz, i).start()
        tile = min(256, rows)
        for i in range(CORES):
            chunk_load(n, zz, i).wait()
            at = zz * CORES + i
            part = jnp.zeros((cols, cols), jnp.float32)
            for t in range(rows // tile):
                part += jnp.dot(
                    pt_buf[t, :, :], chunk_buf[i, pl.ds(t * tile, tile), :],
                    preferred_element_type=jnp.float32)
            part = part.astype(part_buf.dtype)
            owner = at // per_row

            @pl.when(owner == r)
            def _():
                sum_buf[n, r, lax.rem(at, per_row)] = part

            @pl.when(owner != r)
            def _():
                part_buf[n, at] = part
                part_copy(n, at).start()

    def t_store(n):
        return pltpu.make_async_copy(t_buf, t_out.at[n], t_sem)

    def finish_sum(n):
        @pl.when(n > 0)
        def _():
            t_store(n - 1).wait()

        for half in range(per_row):
            total = jnp.zeros((cols, cols), jnp.float32)
            for d in range(1, n_row):
                src = lax.rem(r + d, n_row)
                ref = sum_buf.at[n, src, half]
                pltpu.make_async_remote_copy(
                    ref, ref, part_send.at[n, 0], part_recv.at[n, src, half],
                    (src, c), MESH).wait_recv()
            for src in range(n_row):
                total += sum_buf[n, src, half].astype(jnp.float32)
            t_buf[pl.ds(half * cols, cols), :] = total.T.astype(t_buf.dtype)
        t_store(n).start()

    def wait_mate(item, zz):
        share(item, zz, zz * CORES + 1 - core).wait_recv()

    begin(0)
    send_plane(0)
    send_plane(1)

    def root_hop(h, _):
        arrive(0, h)
        return 0

    lax.fori_loop(0, n_z - 1, root_hop, 0)

    def root_mates(zz, _):
        wait_mate(0, zz)
        return 0

    def kid(n, _):
        item = n + 1

        @pl.when(n < kids - 2)
        def _():
            send_plane(n + 2)

        make_p(n)
        wait_mate(item, z)
        consume(n, z)

        def hop(h, _):
            arrive(item, h)

            @pl.when((h == n_z - 2) & (n < kids - 1))
            def _():
                begin(item + 1)

            low, high = z - 1 - h, z + 1 + h

            @pl.when(low >= 0)
            def _():
                wait_mate(item, low)
                consume(n, low)

            @pl.when(high < n_z)
            def _():
                wait_mate(item, high)
                consume(n, high)

            return 0

        lax.fori_loop(0, n_z - 1, hop, 0)

        @pl.when(n > 0)
        def _():
            finish_sum(n - 1)

        return 0

    begin(jnp.int32(1))
    lax.fori_loop(0, n_z, root_mates, 0)
    lax.fori_loop(0, kids, kid, 0)
    last = jnp.int32(kids - 1)
    finish_sum(last)
    p_store(last).wait()
    t_store(last).wait()

    finish_line(0)

    def drain(n, _):
        finish_line(n + 1)
        for d in range(1, n_row):
            to_row(n, d).wait_send()

        def parts(at, _):
            @pl.when(at // per_row != r)
            def _():
                part_copy(n, at).wait_send()

            return 0

        lax.fori_loop(0, n_col, parts, 0)
        return 0

    lax.fori_loop(0, kids, drain, 0)


def body(n_row, n_col, root_inverse, factor, inverse_diag, structure):
    rows, kids, cols = factor.shape
    offset = lax.axis_index("row") * rows
    row_mask = jnp.repeat(structure, BLK, axis=1)
    local_mask = lax.dynamic_slice_in_dim(row_mask, offset, rows, 1).astype(factor.dtype)
    masked = jnp.transpose(factor, (1, 0, 2)) * local_mask[:, :, None]
    n_z = n_col // CORES
    per_row = rows // cols
    tile = min(256, rows)
    bf16 = jnp.bfloat16
    dma = pltpu.SemaphoreType.DMA
    flops = 4 * kids * rows * cols * rows * n_row
    block = jax.ShapeDtypeStruct((kids, rows, cols), bf16)
    p, total, _, _ = pl.pallas_call(
        functools.partial(kernel, n_row, n_col),
        out_shape=(
            block,
            block,
            jax.ShapeDtypeStruct((kids, n_col, rows, cols), bf16),
            jax.ShapeDtypeStruct((kids, n_row, rows, cols), bf16),
        ),
        in_specs=[pl.BlockSpec(memory_space=pl.ANY)] * 2,
        out_specs=(pl.BlockSpec(memory_space=pl.ANY),) * 4,
        scratch_shapes=[
            pltpu.VMEM((n_col, rows, cols), bf16),
            pltpu.VMEM((n_row, rows, cols), bf16),
            pltpu.VMEM((CORES, rows, cols), bf16),
            pltpu.VMEM((rows, cols), bf16),
            pltpu.VMEM((rows // tile, cols, tile), bf16),
            pltpu.VMEM((kids, n_col, cols, cols), bf16),
            pltpu.VMEM((kids, n_row, per_row, cols, cols), bf16),
            pltpu.VMEM((rows, cols), bf16),
            dma((3,)),
            dma((kids + 1, n_z - 1)),
            dma((kids + 1, n_z - 1)),
            dma((kids + 1, n_z - 1)),
            dma((kids + 1, n_z - 1)),
            dma((kids + 1, n_z)),
            dma((kids + 1, n_z)),
            dma((kids, n_row - 1)),
            dma((kids, n_row - 1)),
            dma((kids, n_col)),
            dma((kids, n_row, per_row)),
            dma((1 + CORES,)),
            dma(()),
            dma(()),
        ],
        compiler_params=pltpu.CompilerParams(
            collective_id=0, has_side_effects=True, vmem_limit_bytes=60 * 1024 * 1024),
        cost_estimate=pl.CostEstimate(
            flops=flops, bytes_accessed=64 * kids * rows * cols, transcendentals=0),
    )(root_inverse, masked)
    ainv_rk = jnp.transpose(p, (1, 0, 2))
    running = jnp.transpose(total, (1, 0, 2)).astype(jnp.float32)
    ainv_kk = (inverse_diag.astype(jnp.float32) - running).astype(bf16)
    return (ainv_rk, ainv_kk)


def solution(mesh):
    return jax.shard_map(
        functools.partial(body, mesh.shape["row"], mesh.shape["col"]),
        mesh=mesh,
        in_specs=(P("row", "col"), P("row", None, "col"), P("row", None, "col"), P()),
        out_specs=(P("row", None, "col"), P("row", None, "col")),
        check_vma=False,
    )
```

time: 744 us -> 673 us (0.905)
  Pallas kernels: 0 us -> 651 us
  waiting for transfers between devices: 635 us -> 0 us
  matrix products: 49.1 us -> 0 us
  local copies, waits for them, and re-layouts: 30.9 us -> 13.7 us
  between operations: 13.8 us -> 0.69 us
    pallas_call x0 -> x1, Pallas kernels: none -> 651 us  [body(): pl.pallas_call(functools.partial(kernel, n_row, n_col), out_shape=(block,...]
    all_gather x3 -> x0, waiting for transfers between devices: 498 us -> none  [the longest x1 268 us: body(): masked_rows = lax.all_gather(masked, 'col', axis=2, tiled=True)]
    reduce_scatter x1 -> x0, waiting for transfers between devices: 135 us -> none  [body(): lax.psum_scatter(jnp.einsum('kni,knj->inj', masked_rows, ainv_rk, preferr...]
    dot_general x2 -> x0, matrix products: 49.1 us -> none  [the longest x1 25.3 us: body(): jnp.einsum('kni,knj->inj', masked_rows, ainv_rk, preferred_element_type=j...]
    unnamed x10 -> x12, local copies, waits for them, and re-layouts: 30.9 us -> 13.7 us
  transfers between devices with their start and end apart: 4 -> 0, of which waited for: 4 -> 0; matrix products, arithmetic and copies ran while one was open for 7% -> 0% of each run, Pallas kernels for 0% -> 0%
where the time goes in v1:
time: 673 us; the launch traced here: 672 us
  Pallas kernels  651 us (97%)
  local copies, waits for them, and re-layouts  13.7 us (2%)
  other arithmetic  7.17 us (1%)
    pallas_call x1, Pallas kernels, body(): pl.pallas_call(functools.partial(kernel, n_row, n_col), out_shape=(block,...  651 us
    unnamed x12, local copies, waits for them, and re-layouts  13.7 us

profile of v1, /device:TPU:7, one launch (start us, length us, event | category | flops | bytes accessed | tf_op | source)
XLA Modules:
  0.0 672.3 jit_solution(1217420208902759614)
XLA Ops:
  0.6 0.0 copy-start
  0.7 0.7 copy-done
  1.3 0.1 broadcast_bitcast_fusion
  1.4 0.1 copy.14
  1.5 5.9 bitcast_multiply_fusion.m_in
  7.4 650.8 %shard_map.59 = (bf16[4,1024,512]{2,1,0:T(8,128)(2,1)}, bf16[4,1024,512]{2,1,0:T(8,128)(2,1)}, bf16[4,8,1024,512]{3,2,1,0:T(8,128)(2,1)}, bf16[4,4,1024,512]{3,2,1,0:T(8,128)(2,1)}) custom-call(bf16[1024,512]{1,0:T(8,128)(2,1)} %root_in.1, bf16[4,1024,512]{2,1,0:T(8,128)(2,1)} %bitcast_multiply_fusion.m_in), custom_call_target="tpu_custom_call" | custom-call | flops 34359738368 | bytes 134217728 | tf_op jit(solution)/shard_map/pallas_call | solution.py:325
  658.2 0.0 copy-start.2
  658.2 0.0 copy-start.3
  658.2 7.6 %copy.8 = bf16[1024,4,512]{2,1,0:T(4,128)(2,1)} copy(bf16[1024,4,512]{2,0,1:T(8,128)(2,1)} %bitcast.12) | data formatting | bytes 8388608
  665.8 0.0 copy-done.2
  665.8 0.0 copy-done.3
  665.8 0.0 copy-start.1
  665.8 1.2 fusion
  667.1 5.2 copy.9
  672.3 0.0 copy-done.1
  (1 shorter events, 0.0 us)
Async XLA Ops:
  0.6 0.7 copy-start
  658.2 7.6 %copy-start.2 = (bf16[1024,4,512]{2,1,0:T(4,128)(2,1)S(1)}, bf16[1024,4,512]{2,1,0:T(4,128)(2,1)}, u32[]{:S(2)}) copy-start(bf16[1024,4,512]{2,1,0:T(4,128)(2,1)} %param.6) | copy-start | bytes 12582916
  658.2 7.6 %copy-start.3 = (bf16[4,1024,512]{2,1,0:T(8,128)(2,1)S(1)}, bf16[4,1024,512]{2,1,0:T(8,128)(2,1)}, u32[]{:S(2)}) copy-start(bf16[4,1024,512]{2,1,0:T(8,128)(2,1)} %get-tuple-element.5) | copy-start | bytes 12582916
  665.8 6.5 copy-start.1

commit v2 on v1

--- a/solution.py
+++ b/solution.py
@@ -175,33 +175,27 @@
         lax.fori_loop(0, rows // tile, one, 0)
         p_store(n).start()
 
-    def chunk_load(n, zz, i):
-        return pltpu.make_async_copy(
-            m_line.at[n, zz * CORES + i], chunk_buf.at[i], load_sem.at[1 + i])
-
-    def consume(n, zz):
-        for i in range(CORES):
-            chunk_load(n, zz, i).start()
+    def consume(n, at):
+        load = pltpu.make_async_copy(m_line.at[n, at], chunk_buf, load_sem.at[1])
+        load.start()
+        load.wait()
         tile = min(256, rows)
-        for i in range(CORES):
-            chunk_load(n, zz, i).wait()
-            at = zz * CORES + i
-            part = jnp.zeros((cols, cols), jnp.float32)
-            for t in range(rows // tile):
-                part += jnp.dot(
-                    pt_buf[t, :, :], chunk_buf[i, pl.ds(t * tile, tile), :],
-                    preferred_element_type=jnp.float32)
-            part = part.astype(part_buf.dtype)
-            owner = at // per_row
-
-            @pl.when(owner == r)
-            def _():
-                sum_buf[n, r, lax.rem(at, per_row)] = part
-
-            @pl.when(owner != r)
-            def _():
-                part_buf[n, at] = part
-                part_copy(n, at).start()
+        part = jnp.zeros((cols, cols), jnp.float32)
+        for t in range(rows // tile):
+            part += jnp.dot(
+                pt_buf[t, :, :], chunk_buf[pl.ds(t * tile, tile), :],
+                preferred_element_type=jnp.float32)
+        part = part.astype(part_buf.dtype)
+        owner = at // per_row
+
+        @pl.when(owner == r)
+        def _():
+            sum_buf[n, r, lax.rem(at, per_row)] = part
+
+        @pl.when(owner != r)
+        def _():
+            part_buf[n, at] = part
+            part_copy(n, at).start()
 
     def t_store(n):
         return pltpu.make_async_copy(t_buf, t_out.at[n], t_sem)
@@ -227,62 +221,66 @@
     def wait_mate(item, zz):
         share(item, zz, zz * CORES + 1 - core).wait_recv()
 
-    begin(0)
-    send_plane(0)
-    send_plane(1)
-
-    def root_hop(h, _):
-        arrive(0, h)
-        return 0
-
-    lax.fori_loop(0, n_z - 1, root_hop, 0)
-
-    def root_mates(zz, _):
-        wait_mate(0, zz)
-        return 0
-
-    def kid(n, _):
-        item = n + 1
-
-        @pl.when(n < kids - 2)
-        def _():
-            send_plane(n + 2)
-
-        make_p(n)
-        wait_mate(item, z)
-        consume(n, z)
-
+    def run_line(item):
         def hop(h, _):
             arrive(item, h)
-
-            @pl.when((h == n_z - 2) & (n < kids - 1))
-            def _():
-                begin(item + 1)
-
-            low, high = z - 1 - h, z + 1 + h
-
-            @pl.when(low >= 0)
-            def _():
-                wait_mate(item, low)
-                consume(n, low)
-
-            @pl.when(high < n_z)
-            def _():
-                wait_mate(item, high)
-                consume(n, high)
-
             return 0
 
         lax.fori_loop(0, n_z - 1, hop, 0)
 
+    def wait_mates(item):
+        def one(zz, _):
+            wait_mate(item, zz)
+            return 0
+
+        lax.fori_loop(0, n_z, one, 0)
+
+    send_plane(0)
+    begin(0)
+    begin(jnp.int32(1))
+    send_plane(1)
+    run_line(0)
+    begin(jnp.int32(2))
+    wait_mates(0)
+    for n in range(2, kids):
+        send_plane(n)
+    make_p(jnp.int32(0))
+    run_line(jnp.int32(1))
+
+    share_of = -(-n_col // (n_z - 1))
+
+    def kid(n, _):
+        @pl.when(n < kids - 2)
+        def _():
+            begin(n + 3)
+
+        wait_mates(n + 1)
+
+        def hop(h, _):
+            def one(i, _):
+                consume(n, lax.rem(i + (r + 1) * per_row, n_col))
+                return 0
+
+            lax.fori_loop(h * share_of, jnp.minimum((h + 1) * share_of, n_col), one, 0)
+
+            @pl.when(n < kids - 1)
+            def _():
+                arrive(n + 2, h)
+
+            return 0
+
+        lax.fori_loop(0, n_z - 1, hop, 0)
+
+        @pl.when(n < kids - 1)
+        def _():
+            make_p(n + 1)
+
         @pl.when(n > 0)
         def _():
             finish_sum(n - 1)
 
         return 0
 
-    begin(jnp.int32(1))
-    lax.fori_loop(0, n_z, root_mates, 0)
     lax.fori_loop(0, kids, kid, 0)
     last = jnp.int32(kids - 1)
     finish_sum(last)
@@ -335,7 +333,7 @@
         scratch_shapes=[
             pltpu.VMEM((n_col, rows, cols), bf16),
             pltpu.VMEM((n_row, rows, cols), bf16),
-            pltpu.VMEM((CORES, rows, cols), bf16),
+            pltpu.VMEM((rows, cols), bf16),
             pltpu.VMEM((rows, cols), bf16),
             pltpu.VMEM((rows // tile, cols, tile), bf16),
             pltpu.VMEM((kids, n_col, cols, cols), bf16),
@@ -352,7 +350,7 @@
             dma((kids, n_row - 1)),
             dma((kids, n_col)),
             dma((kids, n_row, per_row)),
-            dma((1 + CORES,)),
+            dma((2,)),
             dma(()),
             dma(()),
         ],

time: 673 us -> 684 us (1.016)
  Pallas kernels: 651 us -> 658 us
    pallas_call x1, Pallas kernels: 651 us -> 658 us  [body(): pl.pallas_call(functools.partial(kernel, n_row, n_col), out_shape=(block,...]
where the time goes in v2:
time: 684 us; the launch traced here: 680 us
  Pallas kernels  658 us (96%)
  local copies, waits for them, and re-layouts  13.7 us (2%)
  other arithmetic  7.17 us (1%)
    pallas_call x1, Pallas kernels, body(): pl.pallas_call(functools.partial(kernel, n_row, n_col), out_shape=(block,...  658 us

profile of v2, /device:TPU:7, one launch (start us, length us, event | category | flops | bytes accessed | tf_op | source)
XLA Modules:
  0.0 679.8 jit_solution(7816945610987026487)
XLA Ops:
  0.6 0.0 copy-start
  0.7 0.7 copy-done
  1.3 0.1 broadcast_bitcast_fusion
  1.4 0.1 copy.14
  1.5 5.9 bitcast_multiply_fusion.m_in
  7.4 658.3 %shard_map.59 = (bf16[4,1024,512]{2,1,0:T(8,128)(2,1)}, bf16[4,1024,512]{2,1,0:T(8,128)(2,1)}, bf16[4,8,1024,512]{3,2,1,0:T(8,128)(2,1)}, bf16[4,4,1024,512]{3,2,1,0:T(8,128)(2,1)}) custom-call(bf16[1024,512]{1,0:T(8,128)(2,1)} %root_in.1, bf16[4,1024,512]{2,1,0:T(8,128)(2,1)} %bitcast_multiply_fusion.m_in), custom_call_target="tpu_custom_call" | custom-call | flops 34359738368 | bytes 134217728 | tf_op jit(solution)/shard_map/pallas_call | solution.py:323
  665.7 0.0 copy-start.2
  665.7 0.0 copy-start.3
  665.7 7.6 %copy.8 = bf16[1024,4,512]{2,1,0:T(4,128)(2,1)} copy(bf16[1024,4,512]{2,0,1:T(8,128)(2,1)} %bitcast.12) | data formatting | bytes 8388608
  673.3 0.0 copy-done.2
  673.3 0.0 copy-done.3
  673.3 0.0 copy-start.1
  673.3 1.2 fusion
  674.5 5.2 copy.9
  679.8 0.0 copy-done.1
  (1 shorter events, 0.0 us)
Async XLA Ops:
  0.6 0.7 copy-start
  665.7 7.6 %copy-start.2 = (bf16[1024,4,512]{2,1,0:T(4,128)(2,1)S(1)}, bf16[1024,4,512]{2,1,0:T(4,128)(2,1)}, u32[]{:S(2)}) copy-start(bf16[1024,4,512]{2,1,0:T(4,128)(2,1)} %param.6) | copy-start | bytes 12582916
  665.7 7.6 %copy-start.3 = (bf16[4,1024,512]{2,1,0:T(8,128)(2,1)S(1)}, bf16[4,1024,512]{2,1,0:T(8,128)(2,1)}, u32[]{:S(2)}) copy-start(bf16[4,1024,512]{2,1,0:T(8,128)(2,1)} %get-tuple-element.5) | copy-start | bytes 12582916
  673.3 6.5 copy-start.1

commit v3 on v2

--- a/solution.py
+++ b/solution.py
@@ -17,6 +17,7 @@
     root, col_buf, chunk_buf, p_buf, pt_buf, part_buf, sum_buf, t_buf,
     own_sem, up_send, up_recv, down_send, down_recv, mate_send, mate_recv,
     plane_send, plane_recv, part_send, part_recv, load_sem, out_sem, t_sem,
+    flip_buf, flip_send, flip_recv,
 ):
     kids, rows, cols = m_in.shape
     n_z = n_col // CORES
@@ -25,6 +26,15 @@
     z, core = c // CORES, c % CORES
     mate = z * CORES + 1 - core
 
+    def rises(item):
+        return True if isinstance(item, int) else lax.rem(item, 2) == 1
+
+    def sinks(item):
+        return True if isinstance(item, int) else lax.rem(item, 2) == 0
+
+    def held(item, zz):
+        return (zz == z) | ((zz < z) & rises(item)) | ((zz > z) & sinks(item))
+
     barrier = pltpu.get_barrier_semaphore()
 
     def greet(dev):
@@ -36,6 +46,9 @@
 
     for step in (1, n_z - 1):
         greet((r, lax.rem(z + step, n_z) * CORES + core))
+
+    for half in range(per_row):
+        greet((c // per_row, r * per_row + half))
 
     own = [
         pltpu.make_async_copy(root_in, root.at[c], own_sem.at[0]),
@@ -47,7 +60,7 @@
     for copy in own:
         copy.wait()
 
-    pl.semaphore_wait(barrier, n_row + 2)
+    pl.semaphore_wait(barrier, n_row + 2 + per_row)
 
     def slot(item, at):
         return root.at[at] if isinstance(item, int) else m_line.at[item - 1, at]
@@ -68,11 +81,11 @@
             ref, ref, mate_send.at[item, zz], mate_recv.at[item, zz], (r, mate), MESH)
 
     def begin(item):
-        @pl.when(z < n_z - 1)
+        @pl.when((z < n_z - 1) & rises(item))
         def _():
             up(item, 0, c).start()
 
-        @pl.when(z > 0)
+        @pl.when((z > 0) & sinks(item))
         def _():
             down(item, 0, c).start()
 
@@ -81,7 +94,7 @@
     def arrive(item, h):
         low, high = z - 1 - h, z + 1 + h
 
-        @pl.when(low >= 0)
+        @pl.when((low >= 0) & rises(item))
         def _():
             at = low * CORES + core
             up(item, h, at).wait_recv()
@@ -92,7 +105,7 @@
 
             share(item, low, at).start()
 
-        @pl.when(high < n_z)
+        @pl.when((high < n_z) & sinks(item))
         def _():
             at = high * CORES + core
             down(item, h, at).wait_recv()
@@ -105,11 +118,11 @@
 
     def finish_line(item):
         def hop(h, _):
-            @pl.when((z < n_z - 1) & (z - h >= 0))
+            @pl.when((z < n_z - 1) & (z - h >= 0) & rises(item))
             def _():
                 up(item, h, c - h * CORES).wait_send()
 
-            @pl.when((z > 0) & (z + h < n_z))
+            @pl.when((z > 0) & (z + h < n_z) & sinks(item))
             def _():
                 down(item, h, c + h * CORES).wait_send()
 
@@ -118,7 +131,10 @@
         lax.fori_loop(0, n_z - 1, hop, 0)
 
         def mates(zz, _):
-            share(item, zz, zz * CORES + core).wait_send()
+            @pl.when(held(item, zz))
+            def _():
+                share(item, zz, zz * CORES + core).wait_send()
+
             return 0
 
         lax.fori_loop(0, n_z, mates, 0)
@@ -197,26 +213,62 @@
             part_buf[n, at] = part
             part_copy(n, at).start()
 
-    def t_store(n):
-        return pltpu.make_async_copy(t_buf, t_out.at[n], t_sem)
+    def t_store(n, half):
+        at = pl.ds(half * cols, cols)
+        return pltpu.make_async_copy(t_buf.at[n, at], t_out.at[n, at], t_sem.at[n, half])
+
+    def flip(n, half):
+        place = lax.rem(c, per_row)
+        at = pl.ds(pl.multiple_of(place * cols, cols), cols)
+        return pltpu.make_async_remote_copy(
+            flip_buf.at[n, half], t_out.at[n, at], flip_send.at[n, half],
+            flip_recv.at[n, place], (c // per_row, r * per_row + half), MESH)
+
+    def flipped(n, half):
+        return pltpu.make_async_remote_copy(
+            flip_buf.at[n, half], t_out.at[n, pl.ds(half * cols, cols)],
+            flip_send.at[n, half], flip_recv.at[n, half],
+            (c // per_row, r * per_row + half), MESH)
 
     def finish_sum(n):
-        @pl.when(n > 0)
-        def _():
-            t_store(n - 1).wait()
-
         for half in range(per_row):
-            total = jnp.zeros((cols, cols), jnp.float32)
-            for d in range(1, n_row):
-                src = lax.rem(r + d, n_row)
-                ref = sum_buf.at[n, src, half]
-                pltpu.make_async_remote_copy(
-                    ref, ref, part_send.at[n, 0], part_recv.at[n, src, half],
-                    (src, c), MESH).wait_recv()
-            for src in range(n_row):
-                total += sum_buf[n, src, half].astype(jnp.float32)
-            t_buf[pl.ds(half * cols, cols), :] = total.T.astype(t_buf.dtype)
-        t_store(n).start()
+            zz = (r * per_row + half) // CORES
+
+            @pl.when(held(n + 1, zz))
+            def _(half=half, zz=zz):
+                total = jnp.zeros((cols, cols), jnp.float32)
+                for d in range(1, n_row):
+                    src = lax.rem(r + d, n_row)
+                    ref = sum_buf.at[n, src, half]
+                    pltpu.make_async_remote_copy(
+                        ref, ref, part_send.at[n, 0], part_recv.at[n, src, half],
+                        (src, c), MESH).wait_recv()
+                for src in range(n_row):
+                    total += sum_buf[n, src, half].astype(jnp.float32)
+
+                @pl.when(zz != z)
+                def _():
+                    flip_buf[n, half] = total.astype(flip_buf.dtype)
+                    flip(n, half).start()
+
+                t_buf[n, pl.ds(half * cols, cols), :] = total.T.astype(t_buf.dtype)
+                t_store(n, half).start()
+
+    def finish_out(n):
+        for half in range(per_row):
+            zz = (r * per_row + half) // CORES
+
+            @pl.when(held(n + 1, zz))
+            def _(half=half, zz=zz):
+                t_store(n, half).wait()
+
+                @pl.when(zz != z)
+                def _():
+                    flip(n, half).wait_send()
+
+            @pl.when(jnp.logical_not(held(n + 1, zz)))
+            def _(half=half):
+                flipped(n, half).wait_recv()
 
     def wait_mate(item, zz):
         share(item, zz, zz * CORES + 1 - core).wait_recv()
@@ -230,7 +282,10 @@
 
     def wait_mates(item):
         def one(zz, _):
-            wait_mate(item, zz)
+            @pl.when(held(item, zz))
+            def _():
+                wait_mate(item, zz)
+
             return 0
 
         lax.fori_loop(0, n_z, one, 0)
@@ -238,34 +293,44 @@
     send_plane(0)
     begin(0)
     begin(jnp.int32(1))
+    begin(jnp.int32(2))
     send_plane(1)
     run_line(0)
-    begin(jnp.int32(2))
+    for item in range(3, kids + 1):
+        begin(jnp.int32(item))
     wait_mates(0)
     for n in range(2, kids):
         send_plane(n)
     make_p(jnp.int32(0))
-    run_line(jnp.int32(1))
+
+    def first_hop(h, _):
+        arrive(jnp.int32(1), h)
+        arrive(jnp.int32(2), h)
+        return 0
+
+    lax.fori_loop(0, n_z - 1, first_hop, 0)
 
     share_of = -(-n_col // (n_z - 1))
 
     def kid(n, _):
-        @pl.when(n < kids - 2)
-        def _():
-            begin(n + 3)
-
         wait_mates(n + 1)
 
         def hop(h, _):
             def one(i, _):
-                consume(n, lax.rem(i + (r + 1) * per_row, n_col))
+                at = lax.rem(i + (r + 1) * per_row, n_col)
+
+                @pl.when(held(n + 1, at // CORES))
+                def _():
+                    consume(n, at)
+
                 return 0
 
             lax.fori_loop(h * share_of, jnp.minimum((h + 1) * share_of, n_col), one, 0)
 
-            @pl.when(n < kids - 1)
-            def _():
-                arrive(n + 2, h)
+            @pl.when((n < kids - 2) & (lax.rem(n, 2) == 0))
+            def _():
+                arrive(n + 3, h)
+                arrive(n + 4, h)
 
             return 0
 
@@ -285,17 +350,17 @@
     last = jnp.int32(kids - 1)
     finish_sum(last)
     p_store(last).wait()
-    t_store(last).wait()
 
     finish_line(0)
 
     def drain(n, _):
         finish_line(n + 1)
+        finish_out(n)
         for d in range(1, n_row):
             to_row(n, d).wait_send()
 
         def parts(at, _):
-            @pl.when(at // per_row != r)
+            @pl.when((at // per_row != r) & held(n + 1, at // CORES))
             def _():
                 part_copy(n, at).wait_send()
 
@@ -338,7 +403,7 @@
             pltpu.VMEM((rows // tile, cols, tile), bf16),
             pltpu.VMEM((kids, n_col, cols, cols), bf16),
             pltpu.VMEM((kids, n_row, per_row, cols, cols), bf16),
-            pltpu.VMEM((rows, cols), bf16),
+            pltpu.VMEM((kids, rows, cols), bf16),
             dma((3,)),
             dma((kids + 1, n_z - 1)),
             dma((kids + 1, n_z - 1)),
@@ -352,7 +417,10 @@
             dma((kids, n_row, per_row)),
             dma((2,)),
             dma(()),
-            dma(()),
+            dma((kids, per_row)),
+            pltpu.VMEM((kids, per_row, cols, cols), bf16),
+            dma((kids, per_row)),
+            dma((kids, per_row)),
         ],
         compiler_params=pltpu.CompilerParams(
             collective_id=0, has_side_effects=True, vmem_limit_bytes=60 * 1024 * 1024),

time: 684 us -> 693 us (1.013)
  no operation moved by 1% of the time
where the time goes in v3:
time: 693 us; the launch traced here: 683 us
  Pallas kernels  661 us (95%)
  local copies, waits for them, and re-layouts  13.7 us (2%)
  other arithmetic  7.17 us (1%)
    pallas_call x1, Pallas kernels, body(): pl.pallas_call(functools.partial(kernel, n_row, n_col), out_shape=(block,...  661 us

profile of v3, /device:TPU:7, one launch (start us, length us, event | category | flops | bytes accessed | tf_op | source)
XLA Modules:
  0.0 682.8 jit_solution(2701311404884692305)
XLA Ops:
  0.6 0.0 copy-start
  0.7 0.7 copy-done
  1.3 0.1 broadcast_bitcast_fusion
  1.4 0.1 copy.14
  1.5 5.9 bitcast_multiply_fusion.m_in
  7.4 661.2 %shard_map.59 = (bf16[4,1024,512]{2,1,0:T(8,128)(2,1)}, bf16[4,1024,512]{2,1,0:T(8,128)(2,1)}, bf16[4,8,1024,512]{3,2,1,0:T(8,128)(2,1)}, bf16[4,4,1024,512]{3,2,1,0:T(8,128)(2,1)}) custom-call(bf16[1024,512]{1,0:T(8,128)(2,1)} %root_in.1, bf16[4,1024,512]{2,1,0:T(8,128)(2,1)} %bitcast_multiply_fusion.m_in), custom_call_target="tpu_custom_call" | custom-call | flops 34359738368 | bytes 134217728 | tf_op jit(solution)/shard_map/pallas_call | solution.py:388
  668.6 0.0 copy-start.2
  668.6 0.0 copy-start.3
  668.7 7.6 %copy.8 = bf16[1024,4,512]{2,1,0:T(4,128)(2,1)} copy(bf16[1024,4,512]{2,0,1:T(8,128)(2,1)} %bitcast.12) | data formatting | bytes 8388608
  676.2 0.0 copy-done.2
  676.2 0.0 copy-done.3
  676.2 0.0 copy-start.1
  676.3 1.2 fusion
  677.5 5.2 copy.9
  682.8 0.0 copy-done.1
  (1 shorter events, 0.0 us)
Async XLA Ops:
  0.6 0.7 copy-start
  668.6 7.6 %copy-start.2 = (bf16[1024,4,512]{2,1,0:T(4,128)(2,1)S(1)}, bf16[1024,4,512]{2,1,0:T(4,128)(2,1)}, u32[]{:S(2)}) copy-start(bf16[1024,4,512]{2,1,0:T(4,128)(2,1)} %param.6) | copy-start | bytes 12582916
  668.6 7.6 %copy-start.3 = (bf16[4,1024,512]{2,1,0:T(8,128)(2,1)S(1)}, bf16[4,1024,512]{2,1,0:T(8,128)(2,1)}, u32[]{:S(2)}) copy-start(bf16[4,1024,512]{2,1,0:T(8,128)(2,1)} %get-tuple-element.5) | copy-start | bytes 12582916
  676.2 6.5 copy-start.1
